TPU v7x, 32 devices: a whole 2x2x4 slice. The times are simulated.
32 devices in a mesh: layer: 8 (over z, y), plane: 4 (over x, core).
Axes of the slice: x: 2, y: 2, z: 4, core: 2. Of those that a mesh axis runs over, the one named last changes fastest.
Arguments:
- rhs_field: float32 [8, 2, 4, 32, 1024], P('layer', None, None, None, 'plane'), may hold values from -6 to 6
- panel_inverse: bfloat16 [8, 1024, 2048], P('layer'), may hold values from -1 to 1
- coupling: float32 [8, 2, 4, 32], P('layer', None, None, 'plane'), may hold values from -0.98 to 0.98, as said below
Outputs:
- sweep_field: float32 [8, 2, 4, 32, 1024], P('layer', None, None, None, 'plane')
Inputs may be any that keep to these rules, and one draw needn't show every extreme that they name: Every complex coupling has modulus at most 0.98.
All inputs are finite; a program needn't handle non-finite values.
Results may differ from a plain program's by a relative error of at most 0.025.
Values may be sent and summed in bfloat16 or wider, within the bound.
A program may use at most 64 MiB of HBM per device.

v0:
```python
import jax
import jax.numpy as jnp
from jax import lax
from jax.sharding import PartitionSpec as P


def from_behind(value, axis, steps):
    count = lax.axis_size(axis)
    first, last = (max(0, -steps), min(count, count - steps))
    return lax.ppermute(value, axis, [(source, source + steps) for source in range(first, last)])


def complex_product(rows, inverse, width):
    flat = rows.reshape(-1, width)
    product = jnp.dot(flat, inverse, preferred_element_type=jnp.float32)
    product = product.reshape(rows.shape[:-1] + (2 * width,))
    real = product[0, ..., :width] - product[1, ..., width:]
    imag = product[0, ..., width:] + product[1, ..., :width]
    return jnp.stack([real, imag])


def twist(factor, field):
    real = factor[0] * field[0] - factor[1] * field[1]
    imag = factor[0] * field[1] + factor[1] * field[0]
    return jnp.stack([real, imag])


def body(rhs_field, panel_inverse, coupling):
    lines = lax.all_to_all(rhs_field, "plane", split_axis=3, concat_axis=4, tiled=True)[0]
    inverse = panel_inverse[0]
    factors = coupling[0][..., None]
    width = inverse.shape[0]
    rhs_count = lines.shape[1]
    per_block = 2
    blocks = rhs_count // per_block
    layers = lax.axis_size("layer")
    place = lax.axis_index("layer")
    sections = layers + blocks - 1
    block_shape = (2, per_block) + lines.shape[2:]
    empty_store = jnp.zeros(lines.shape, jnp.float32)
    empty_block = jnp.zeros(block_shape, jnp.bfloat16)

    def locate(offset):
        valid = (offset >= 0) & (offset < blocks)
        start = jnp.clip(offset, 0, blocks - 1) * per_block
        return (valid, start)

    def forward(section, carry):
        store, outgoing = carry
        incoming = from_behind(outgoing, "layer", 1)
        valid, start = locate(section - place)
        source = lax.dynamic_slice_in_dim(lines, start, per_block, 1)
        factor = lax.dynamic_slice_in_dim(factors, start, per_block, 1)
        mixed = (source + twist(factor, incoming.astype(jnp.float32))).astype(jnp.bfloat16)
        result = complex_product(mixed, inverse, width)
        previous = lax.dynamic_slice_in_dim(store, start, per_block, 1)
        store = lax.dynamic_update_slice_in_dim(store, jnp.where(valid, result, previous), start, 1)
        return (store, result.astype(jnp.bfloat16))

    forward_store, _ = lax.fori_loop(0, sections, forward, (empty_store, empty_block))

    def backward(section, carry):
        store, outgoing = carry
        incoming = from_behind(outgoing, "layer", -1)
        valid, start = locate(section - (layers - 1 - place))
        starting_position = lax.dynamic_slice_in_dim(forward_store, start, per_block, 1)
        factor = lax.dynamic_slice_in_dim(factors, start, per_block, 1)
        result = starting_position + complex_product(incoming, inverse, width)
        previous = lax.dynamic_slice_in_dim(store, start, per_block, 1)
        store = lax.dynamic_update_slice_in_dim(store, jnp.where(valid, result, previous), start, 1)
        return (store, twist(factor, result).astype(jnp.bfloat16))

    backward_store, _ = lax.fori_loop(0, sections, backward, (empty_store, empty_block))
    return lax.all_to_all(backward_store[None], "plane", split_axis=4, concat_axis=3, tiled=True)


def solution(mesh):
    in_specs = (
        P("layer", None, None, None, "plane"),
        P("layer", None, None),
        P("layer", None, None, "plane"),
    )
    out_specs = P("layer", None, None, None, "plane")
    return jax.shard_map(body, mesh=mesh, in_specs=in_specs, out_specs=out_specs, check_vma=False)
```

profile of v0, /device:TPU:0, one launch (start us, length us, event | category | flops | bytes accessed | tf_op | source)
XLA Modules:
  0.0 231.6 jit_solution(2552372839723255374)
XLA Ops:
  0.0 1.8 copy.6
  1.8 4.2 %all-to-all-start = ((f32[1,2,4,32,256]{4,2,1,0,3:T(4,128)}), f32[1,2,4,32,256]{4,2,1,0,3:T(4,128)S(1)}, u32[]{:S(2)}, u32[]{:S(2)}) async-start(f32[1,2,4,32,256]{4,2,1,0,3:T(4,128)} %copy.6), calls=%async_computation | async-start | bytes 524288 | tf_op jit(solution)/shard_map/all_to_all | solution.py:29
  6.0 6.0 %all-to-all-done = f32[1,2,4,32,256]{4,2,1,0,3:T(4,128)S(1)} async-done(((f32[1,2,4,32,256]{4,2,1,0,3:T(4,128)}), f32[1,2,4,32,256]{4,2,1,0,3:T(4,128)S(1)}, u32[]{:S(2)}, u32[]{:S(2)}) %all-to-all-start) | async-done | bytes 262176 | tf_op jit(solution)/shard_map/all_to_all | solution.py:29
  12.2 89.9 %while.34 = (s32[]{:T(128)}, f32[2,4,8,1024]{3,2,1,0:T(8,128)S(1)}, bf16[2,2,8,1024]{3,2,1,0:T(8,128)(2,1)S(1)}, s32[]{:T(128)}, f32[2,4,8,1024]{3,2,1,0:T(8,128...) while((s32[]{:T(128)}, f32[2,4,8,1024]{3,2,1,0:T(8,128)S(1)}, ...), condition=%wide.region_1.2_spmd.clone, body=%wide.region_0.1_spmd.clone.sunk | while | flops 134610960 | bytes 6554283 | solution.py:60
  12.2 4.0 %collective-permute-start.1 = (bf16[2,2,8,1024]{3,2,1,0:T(8,128)(2,1)S(1)}, bf16[2,2,8,1024]{3,2,1,0:T(8,128)(2,1)S(1)}, u32[]{:S(2)}, u32[]{:S(2)}) collective-permute-start(bf16[2,2,8,1024]{3,2,1,0:T(8,128)(2,1)S(1)} %broadcast_select_fusion.2), channel_id=1, source_target_pairs={{0,4},{4,8},{8,12},{12,16},{16,20},{20,24},{24,28},{1,5},{5,9},{9,... | collective-permute-start | bytes 196616 | tf_op jit(solution)/shard_map/while/body/eval_jaxpr/ppermute | solution.py:10
  18.3 3.0 %fusion.30 = f32[2,2,8,2048]{3,2,1,0:T(8,128)S(1)} fusion(bf16[1024,2048]{1,0:T(8,128)(2,1)} %get-tuple-element.539, f32[1,2,8,1024]{3,2,1,0:T(8,128)S(1)} %get-tuple-element.505, f32[1,2,8,1024]{3,2,1,0:T(8,128)S(1)} %get-tuple-element.506, f32[2,4,8,1024]{3,2,1,0:T(8,128)S(1)} %get-tuple-element.537, s32[]{:T(128)S(6)} %select_n.74), kind=kOutput, calls=%fused_computation.13.clone.1 | convolution fusion | flops 134316032 | bytes 4718596 | tf_op jit(solution)/shard_map/while/body/eval_jaxpr/dot_general | solution.py:15
  21.4 4.3 %collective-permute-start.1 = (bf16[2,2,8,1024]{3,2,1,0:T(8,128)(2,1)S(1)}, bf16[2,2,8,1024]{3,2,1,0:T(8,128)(2,1)S(1)}, u32[]{:S(2)}, u32[]{:S(2)}) collective-permute-start(bf16[2,2,8,1024]{3,2,1,0:T(8,128)(2,1)S(1)} %broadcast_select_fusion.2), channel_id=1, source_target_pairs={{0,4},{4,8},{8,12},{12,16},{16,20},{20,24},{24,28},{1,5},{5,9},{9,... | collective-permute-start | bytes 196616 | tf_op jit(solution)/shard_map/while/body/eval_jaxpr/ppermute | solution.py:10
  27.6 3.0 %fusion.30 = f32[2,2,8,2048]{3,2,1,0:T(8,128)S(1)} fusion(bf16[1024,2048]{1,0:T(8,128)(2,1)} %get-tuple-element.539, f32[1,2,8,1024]{3,2,1,0:T(8,128)S(1)} %get-tuple-element.505, f32[1,2,8,1024]{3,2,1,0:T(8,128)S(1)} %get-tuple-element.506, f32[2,4,8,1024]{3,2,1,0:T(8,128)S(1)} %get-tuple-element.537, s32[]{:T(128)S(6)} %select_n.74), kind=kOutput, calls=%fused_computation.13.clone.1 | convolution fusion | flops 134316032 | bytes 4718596 | tf_op jit(solution)/shard_map/while/body/eval_jaxpr/dot_general | solution.py:15
  30.7 4.3 %collective-permute-start.1 = (bf16[2,2,8,1024]{3,2,1,0:T(8,128)(2,1)S(1)}, bf16[2,2,8,1024]{3,2,1,0:T(8,128)(2,1)S(1)}, u32[]{:S(2)}, u32[]{:S(2)}) collective-permute-start(bf16[2,2,8,1024]{3,2,1,0:T(8,128)(2,1)S(1)} %broadcast_select_fusion.2), channel_id=1, source_target_pairs={{0,4},{4,8},{8,12},{12,16},{16,20},{20,24},{24,28},{1,5},{5,9},{9,... | collective-permute-start | bytes 196616 | tf_op jit(solution)/shard_map/while/body/eval_jaxpr/ppermute | solution.py:10
  37.1 3.0 %fusion.30 = f32[2,2,8,2048]{3,2,1,0:T(8,128)S(1)} fusion(bf16[1024,2048]{1,0:T(8,128)(2,1)} %get-tuple-element.539, f32[1,2,8,1024]{3,2,1,0:T(8,128)S(1)} %get-tuple-element.505, f32[1,2,8,1024]{3,2,1,0:T(8,128)S(1)} %get-tuple-element.506, f32[2,4,8,1024]{3,2,1,0:T(8,128)S(1)} %get-tuple-element.537, s32[]{:T(128)S(6)} %select_n.74), kind=kOutput, calls=%fused_computation.13.clone.1 | convolution fusion | flops 134316032 | bytes 4718596 | tf_op jit(solution)/shard_map/while/body/eval_jaxpr/dot_general | solution.py:15
  40.2 5.2 %collective-permute-start.1 = (bf16[2,2,8,1024]{3,2,1,0:T(8,128)(2,1)S(1)}, bf16[2,2,8,1024]{3,2,1,0:T(8,128)(2,1)S(1)}, u32[]{:S(2)}, u32[]{:S(2)}) collective-permute-start(bf16[2,2,8,1024]{3,2,1,0:T(8,128)(2,1)S(1)} %broadcast_select_fusion.2), channel_id=1, source_target_pairs={{0,4},{4,8},{8,12},{12,16},{16,20},{20,24},{24,28},{1,5},{5,9},{9,... | collective-permute-start | bytes 196616 | tf_op jit(solution)/shard_map/while/body/eval_jaxpr/ppermute | solution.py:10
  47.3 3.0 %fusion.30 = f32[2,2,8,2048]{3,2,1,0:T(8,128)S(1)} fusion(bf16[1024,2048]{1,0:T(8,128)(2,1)} %get-tuple-element.539, f32[1,2,8,1024]{3,2,1,0:T(8,128)S(1)} %get-tuple-element.505, f32[1,2,8,1024]{3,2,1,0:T(8,128)S(1)} %get-tuple-element.506, f32[2,4,8,1024]{3,2,1,0:T(8,128)S(1)} %get-tuple-element.537, s32[]{:T(128)S(6)} %select_n.74), kind=kOutput, calls=%fused_computation.13.clone.1 | convolution fusion | flops 134316032 | bytes 4718596 | tf_op jit(solution)/shard_map/while/body/eval_jaxpr/dot_general | solution.py:15
  50.4 5.2 %collective-permute-start.1 = (bf16[2,2,8,1024]{3,2,1,0:T(8,128)(2,1)S(1)}, bf16[2,2,8,1024]{3,2,1,0:T(8,128)(2,1)S(1)}, u32[]{:S(2)}, u32[]{:S(2)}) collective-permute-start(bf16[2,2,8,1024]{3,2,1,0:T(8,128)(2,1)S(1)} %broadcast_select_fusion.2), channel_id=1, source_target_pairs={{0,4},{4,8},{8,12},{12,16},{16,20},{20,24},{24,28},{1,5},{5,9},{9,... | collective-permute-start | bytes 196616 | tf_op jit(solution)/shard_map/while/body/eval_jaxpr/ppermute | solution.py:10
  57.6 3.0 %fusion.30 = f32[2,2,8,2048]{3,2,1,0:T(8,128)S(1)} fusion(bf16[1024,2048]{1,0:T(8,128)(2,1)} %get-tuple-element.539, f32[1,2,8,1024]{3,2,1,0:T(8,128)S(1)} %get-tuple-element.505, f32[1,2,8,1024]{3,2,1,0:T(8,128)S(1)} %get-tuple-element.506, f32[2,4,8,1024]{3,2,1,0:T(8,128)S(1)} %get-tuple-element.537, s32[]{:T(128)S(6)} %select_n.74), kind=kOutput, calls=%fused_computation.13.clone.1 | convolution fusion | flops 134316032 | bytes 4718596 | tf_op jit(solution)/shard_map/while/body/eval_jaxpr/dot_general | solution.py:15
  60.7 5.2 %collective-permute-start.1 = (bf16[2,2,8,1024]{3,2,1,0:T(8,128)(2,1)S(1)}, bf16[2,2,8,1024]{3,2,1,0:T(8,128)(2,1)S(1)}, u32[]{:S(2)}, u32[]{:S(2)}) collective-permute-start(bf16[2,2,8,1024]{3,2,1,0:T(8,128)(2,1)S(1)} %broadcast_select_fusion.2), channel_id=1, source_target_pairs={{0,4},{4,8},{8,12},{12,16},{16,20},{20,24},{24,28},{1,5},{5,9},{9,... | collective-permute-start | bytes 196616 | tf_op jit(solution)/shard_map/while/body/eval_jaxpr/ppermute | solution.py:10
  67.9 3.0 %fusion.30 = f32[2,2,8,2048]{3,2,1,0:T(8,128)S(1)} fusion(bf16[1024,2048]{1,0:T(8,128)(2,1)} %get-tuple-element.539, f32[1,2,8,1024]{3,2,1,0:T(8,128)S(1)} %get-tuple-element.505, f32[1,2,8,1024]{3,2,1,0:T(8,128)S(1)} %get-tuple-element.506, f32[2,4,8,1024]{3,2,1,0:T(8,128)S(1)} %get-tuple-element.537, s32[]{:T(128)S(6)} %select_n.74), kind=kOutput, calls=%fused_computation.13.clone.1 | convolution fusion | flops 134316032 | bytes 4718596 | tf_op jit(solution)/shard_map/while/body/eval_jaxpr/dot_general | solution.py:15
  71.0 5.2 %collective-permute-start.1 = (bf16[2,2,8,1024]{3,2,1,0:T(8,128)(2,1)S(1)}, bf16[2,2,8,1024]{3,2,1,0:T(8,128)(2,1)S(1)}, u32[]{:S(2)}, u32[]{:S(2)}) collective-permute-start(bf16[2,2,8,1024]{3,2,1,0:T(8,128)(2,1)S(1)} %broadcast_select_fusion.2), channel_id=1, source_target_pairs={{0,4},{4,8},{8,12},{12,16},{16,20},{20,24},{24,28},{1,5},{5,9},{9,... | collective-permute-start | bytes 196616 | tf_op jit(solution)/shard_map/while/body/eval_jaxpr/ppermute | solution.py:10
  78.1 3.0 %fusion.30 = f32[2,2,8,2048]{3,2,1,0:T(8,128)S(1)} fusion(bf16[1024,2048]{1,0:T(8,128)(2,1)} %get-tuple-element.539, f32[1,2,8,1024]{3,2,1,0:T(8,128)S(1)} %get-tuple-element.505, f32[1,2,8,1024]{3,2,1,0:T(8,128)S(1)} %get-tuple-element.506, f32[2,4,8,1024]{3,2,1,0:T(8,128)S(1)} %get-tuple-element.537, s32[]{:T(128)S(6)} %select_n.74), kind=kOutput, calls=%fused_computation.13.clone.1 | convolution fusion | flops 134316032 | bytes 4718596 | tf_op jit(solution)/shard_map/while/body/eval_jaxpr/dot_general | solution.py:15
  81.2 5.2 %collective-permute-start.1 = (bf16[2,2,8,1024]{3,2,1,0:T(8,128)(2,1)S(1)}, bf16[2,2,8,1024]{3,2,1,0:T(8,128)(2,1)S(1)}, u32[]{:S(2)}, u32[]{:S(2)}) collective-permute-start(bf16[2,2,8,1024]{3,2,1,0:T(8,128)(2,1)S(1)} %broadcast_select_fusion.2), channel_id=1, source_target_pairs={{0,4},{4,8},{8,12},{12,16},{16,20},{20,24},{24,28},{1,5},{5,9},{9,... | collective-permute-start | bytes 196616 | tf_op jit(solution)/shard_map/while/body/eval_jaxpr/ppermute | solution.py:10
  87.1 1.7 collective-permute-done.1
  88.9 3.0 %fusion.30 = f32[2,2,8,2048]{3,2,1,0:T(8,128)S(1)} fusion(bf16[1024,2048]{1,0:T(8,128)(2,1)} %get-tuple-element.539, f32[1,2,8,1024]{3,2,1,0:T(8,128)S(1)} %get-tuple-element.505, f32[1,2,8,1024]{3,2,1,0:T(8,128)S(1)} %get-tuple-element.506, f32[2,4,8,1024]{3,2,1,0:T(8,128)S(1)} %get-tuple-element.537, s32[]{:T(128)S(6)} %select_n.74), kind=kOutput, calls=%fused_computation.13.clone.1 | convolution fusion | flops 134316032 | bytes 4718596 | tf_op jit(solution)/shard_map/while/body/eval_jaxpr/dot_general | solution.py:15
  92.0 4.9 %collective-permute-start.1 = (bf16[2,2,8,1024]{3,2,1,0:T(8,128)(2,1)S(1)}, bf16[2,2,8,1024]{3,2,1,0:T(8,128)(2,1)S(1)}, u32[]{:S(2)}, u32[]{:S(2)}) collective-permute-start(bf16[2,2,8,1024]{3,2,1,0:T(8,128)(2,1)S(1)} %broadcast_select_fusion.2), channel_id=1, source_target_pairs={{0,4},{4,8},{8,12},{12,16},{16,20},{20,24},{24,28},{1,5},{5,9},{9,... | collective-permute-start | bytes 196616 | tf_op jit(solution)/shard_map/while/body/eval_jaxpr/ppermute | solution.py:10
  99.0 3.0 %fusion.30 = f32[2,2,8,2048]{3,2,1,0:T(8,128)S(1)} fusion(bf16[1024,2048]{1,0:T(8,128)(2,1)} %get-tuple-element.539, f32[1,2,8,1024]{3,2,1,0:T(8,128)S(1)} %get-tuple-element.505, f32[1,2,8,1024]{3,2,1,0:T(8,128)S(1)} %get-tuple-element.506, f32[2,4,8,1024]{3,2,1,0:T(8,128)S(1)} %get-tuple-element.537, s32[]{:T(128)S(6)} %select_n.74), kind=kOutput, calls=%fused_computation.13.clone.1 | convolution fusion | flops 134316032 | bytes 4718596 | tf_op jit(solution)/shard_map/while/body/eval_jaxpr/dot_general | solution.py:15
  102.1 93.4 %while.33 = (s32[]{:T(128)}, f32[2,4,8,1024]{3,2,1,0:T(8,128)S(1)}, bf16[2,2,8,1024]{3,2,1,0:T(8,128)(2,1)S(1)}, s32[]{:T(128)}, f32[2,4,8,1024]{3,2,1,0:T(8,128...) while((s32[]{:T(128)}, f32[2,4,8,1024]{3,2,1,0:T(8,128)S(1)}, ...), condition=%wide.region_3.4_spmd, body=%wide.region_2.3_spmd.sunk | while | flops 134512656 | bytes 6161053 | solution.py:73
  104.1 5.5 %collective-permute-done = bf16[2,2,8,1024]{3,2,1,0:T(8,128)(2,1)S(1)} collective-permute-done((bf16[2,2,8,1024]{3,2,1,0:T(8,128)(2,1)S(1)}, bf16[2,2,8,1024]{3,2,1,0:T(8,128)(2,1)S(1)}, u32[]{:S(2)}, u32[]{:S(2)}) %collective-permute-start) | collective-permute-done | bytes 65568 | tf_op jit(solution)/shard_map/while/body/eval_jaxpr/ppermute | solution.py:10
  109.6 3.0 %fusion.25 = f32[2,2,8,2048]{3,2,1,0:T(8,128)S(1)} fusion(bf16[2,2,8,1024]{3,2,1,0:T(8,128)(2,1)S(1)} %collective-permute-done, bf16[1024,2048]{1,0:T(8,128)(2,1)} %get-tuple-element.574), kind=kOutput, calls=%fused_computation.clone.1 | convolution fusion | flops 134217728 | bytes 4521984 | tf_op jit(solution)/shard_map/while/body/eval_jaxpr/dot_general | solution.py:15
  114.8 5.4 %collective-permute-done = bf16[2,2,8,1024]{3,2,1,0:T(8,128)(2,1)S(1)} collective-permute-done((bf16[2,2,8,1024]{3,2,1,0:T(8,128)(2,1)S(1)}, bf16[2,2,8,1024]{3,2,1,0:T(8,128)(2,1)S(1)}, u32[]{:S(2)}, u32[]{:S(2)}) %collective-permute-start) | collective-permute-done | bytes 65568 | tf_op jit(solution)/shard_map/while/body/eval_jaxpr/ppermute | solution.py:10
  120.2 3.0 %fusion.25 = f32[2,2,8,2048]{3,2,1,0:T(8,128)S(1)} fusion(bf16[2,2,8,1024]{3,2,1,0:T(8,128)(2,1)S(1)} %collective-permute-done, bf16[1024,2048]{1,0:T(8,128)(2,1)} %get-tuple-element.574), kind=kOutput, calls=%fused_computation.clone.1 | convolution fusion | flops 134217728 | bytes 4521984 | tf_op jit(solution)/shard_map/while/body/eval_jaxpr/dot_general | solution.py:15
  125.4 5.0 %collective-permute-done = bf16[2,2,8,1024]{3,2,1,0:T(8,128)(2,1)S(1)} collective-permute-done((bf16[2,2,8,1024]{3,2,1,0:T(8,128)(2,1)S(1)}, bf16[2,2,8,1024]{3,2,1,0:T(8,128)(2,1)S(1)}, u32[]{:S(2)}, u32[]{:S(2)}) %collective-permute-start) | collective-permute-done | bytes 65568 | tf_op jit(solution)/shard_map/while/body/eval_jaxpr/ppermute | solution.py:10
  130.5 3.0 %fusion.25 = f32[2,2,8,2048]{3,2,1,0:T(8,128)S(1)} fusion(bf16[2,2,8,1024]{3,2,1,0:T(8,128)(2,1)S(1)} %collective-permute-done, bf16[1024,2048]{1,0:T(8,128)(2,1)} %get-tuple-element.574), kind=kOutput, calls=%fused_computation.clone.1 | convolution fusion | flops 134217728 | bytes 4521984 | tf_op jit(solution)/shard_map/while/body/eval_jaxpr/dot_general | solution.py:15
  135.7 5.0 %collective-permute-done = bf16[2,2,8,1024]{3,2,1,0:T(8,128)(2,1)S(1)} collective-permute-done((bf16[2,2,8,1024]{3,2,1,0:T(8,128)(2,1)S(1)}, bf16[2,2,8,1024]{3,2,1,0:T(8,128)(2,1)S(1)}, u32[]{:S(2)}, u32[]{:S(2)}) %collective-permute-start) | collective-permute-done | bytes 65568 | tf_op jit(solution)/shard_map/while/body/eval_jaxpr/ppermute | solution.py:10
  140.7 3.0 %fusion.25 = f32[2,2,8,2048]{3,2,1,0:T(8,128)S(1)} fusion(bf16[2,2,8,1024]{3,2,1,0:T(8,128)(2,1)S(1)} %collective-permute-done, bf16[1024,2048]{1,0:T(8,128)(2,1)} %get-tuple-element.574), kind=kOutput, calls=%fused_computation.clone.1 | convolution fusion | flops 134217728 | bytes 4521984 | tf_op jit(solution)/shard_map/while/body/eval_jaxpr/dot_general | solution.py:15
  145.9 5.0 %collective-permute-done = bf16[2,2,8,1024]{3,2,1,0:T(8,128)(2,1)S(1)} collective-permute-done((bf16[2,2,8,1024]{3,2,1,0:T(8,128)(2,1)S(1)}, bf16[2,2,8,1024]{3,2,1,0:T(8,128)(2,1)S(1)}, u32[]{:S(2)}, u32[]{:S(2)}) %collective-permute-start) | collective-permute-done | bytes 65568 | tf_op jit(solution)/shard_map/while/body/eval_jaxpr/ppermute | solution.py:10
  150.9 3.0 %fusion.25 = f32[2,2,8,2048]{3,2,1,0:T(8,128)S(1)} fusion(bf16[2,2,8,1024]{3,2,1,0:T(8,128)(2,1)S(1)} %collective-permute-done, bf16[1024,2048]{1,0:T(8,128)(2,1)} %get-tuple-element.574), kind=kOutput, calls=%fused_computation.clone.1 | convolution fusion | flops 134217728 | bytes 4521984 | tf_op jit(solution)/shard_map/while/body/eval_jaxpr/dot_general | solution.py:15
  156.1 5.0 %collective-permute-done = bf16[2,2,8,1024]{3,2,1,0:T(8,128)(2,1)S(1)} collective-permute-done((bf16[2,2,8,1024]{3,2,1,0:T(8,128)(2,1)S(1)}, bf16[2,2,8,1024]{3,2,1,0:T(8,128)(2,1)S(1)}, u32[]{:S(2)}, u32[]{:S(2)}) %collective-permute-start) | collective-permute-done | bytes 65568 | tf_op jit(solution)/shard_map/while/body/eval_jaxpr/ppermute | solution.py:10
  161.2 3.0 %fusion.25 = f32[2,2,8,2048]{3,2,1,0:T(8,128)S(1)} fusion(bf16[2,2,8,1024]{3,2,1,0:T(8,128)(2,1)S(1)} %collective-permute-done, bf16[1024,2048]{1,0:T(8,128)(2,1)} %get-tuple-element.574), kind=kOutput, calls=%fused_computation.clone.1 | convolution fusion | flops 134217728 | bytes 4521984 | tf_op jit(solution)/shard_map/while/body/eval_jaxpr/dot_general | solution.py:15
  166.4 5.2 %collective-permute-done = bf16[2,2,8,1024]{3,2,1,0:T(8,128)(2,1)S(1)} collective-permute-done((bf16[2,2,8,1024]{3,2,1,0:T(8,128)(2,1)S(1)}, bf16[2,2,8,1024]{3,2,1,0:T(8,128)(2,1)S(1)}, u32[]{:S(2)}, u32[]{:S(2)}) %collective-permute-start) | collective-permute-done | bytes 65568 | tf_op jit(solution)/shard_map/while/body/eval_jaxpr/ppermute | solution.py:10
  171.6 3.0 %fusion.25 = f32[2,2,8,2048]{3,2,1,0:T(8,128)S(1)} fusion(bf16[2,2,8,1024]{3,2,1,0:T(8,128)(2,1)S(1)} %collective-permute-done, bf16[1024,2048]{1,0:T(8,128)(2,1)} %get-tuple-element.574), kind=kOutput, calls=%fused_computation.clone.1 | convolution fusion | flops 134217728 | bytes 4521984 | tf_op jit(solution)/shard_map/while/body/eval_jaxpr/dot_general | solution.py:15
  176.8 5.2 %collective-permute-done = bf16[2,2,8,1024]{3,2,1,0:T(8,128)(2,1)S(1)} collective-permute-done((bf16[2,2,8,1024]{3,2,1,0:T(8,128)(2,1)S(1)}, bf16[2,2,8,1024]{3,2,1,0:T(8,128)(2,1)S(1)}, u32[]{:S(2)}, u32[]{:S(2)}) %collective-permute-start) | collective-permute-done | bytes 65568 | tf_op jit(solution)/shard_map/while/body/eval_jaxpr/ppermute | solution.py:10
  182.1 3.0 %fusion.25 = f32[2,2,8,2048]{3,2,1,0:T(8,128)S(1)} fusion(bf16[2,2,8,1024]{3,2,1,0:T(8,128)(2,1)S(1)} %collective-permute-done, bf16[1024,2048]{1,0:T(8,128)(2,1)} %get-tuple-element.574), kind=kOutput, calls=%fused_computation.clone.1 | convolution fusion | flops 134217728 | bytes 4521984 | tf_op jit(solution)/shard_map/while/body/eval_jaxpr/dot_general | solution.py:15
  187.3 5.0 %collective-permute-done = bf16[2,2,8,1024]{3,2,1,0:T(8,128)(2,1)S(1)} collective-permute-done((bf16[2,2,8,1024]{3,2,1,0:T(8,128)(2,1)S(1)}, bf16[2,2,8,1024]{3,2,1,0:T(8,128)(2,1)S(1)}, u32[]{:S(2)}, u32[]{:S(2)}) %collective-permute-start) | collective-permute-done | bytes 65568 | tf_op jit(solution)/shard_map/while/body/eval_jaxpr/ppermute | solution.py:10
  192.3 3.0 %fusion.25 = f32[2,2,8,2048]{3,2,1,0:T(8,128)S(1)} fusion(bf16[2,2,8,1024]{3,2,1,0:T(8,128)(2,1)S(1)} %collective-permute-done, bf16[1024,2048]{1,0:T(8,128)(2,1)} %get-tuple-element.574), kind=kOutput, calls=%fused_computation.clone.1 | convolution fusion | flops 134217728 | bytes 4521984 | tf_op jit(solution)/shard_map/while/body/eval_jaxpr/dot_general | solution.py:15
  195.5 3.1 %copy.10 = f32[2,4,8,1024]{2,1,0,3:T(4,128)} copy(f32[2,4,8,1024]{3,2,1,0:T(8,128)S(1)} %get-tuple-element.300) | data formatting | bytes 524288 | tf_op jit(solution)/shard_map/while | solution.py:73
  198.6 4.9 %bitcast_bitcast_fusion = f32[1024,1,2,4,8]{4,3,2,1,0:T(4,128)} fusion(f32[2,4,8,1024]{2,1,0,3:T(4,128)} %copy.10), kind=kLoop, calls=%fused_computation.31 | loop fusion | bytes 524288
  203.4 6.5 %reshape.23 = f32[4,1,16384]{2,1,0:T(1,128)S(1)} reshape(f32[1024,1,2,4,8]{4,3,2,1,0:T(4,128)} %bitcast_bitcast_fusion) | data formatting | bytes 524288
  209.9 8.4 %all_to_all.33 = f32[4,1,16384]{2,1,0:T(1,128)S(1)} all-to-all(f32[4,1,16384]{2,1,0:T(1,128)S(1)} %reshape.23), channel_id=1, replica_groups=mesh['layer'=8,'plane'=4] {'plane'}, dimensions={0} | all-to-all | bytes 524288 | tf_op jit(solution)/shard_map/all_to_all | solution.py:74
  220.2 7.0 %reshape.24 = f32[1024,1,2,4,8]{4,3,2,1,0:T(4,128)} reshape(f32[4,16384]{1,0:T(4,128)S(1)} %reduce) | data formatting | bytes 524288
  227.2 4.4 %copy.11 = f32[1,2,4,4,8,256]{5,4,3,2,1,0:T(8,128)} copy(f32[1,2,4,4,8,256]{4,2,1,5,3,0:T(4,128)} %bitcast.48) | data formatting | bytes 524288 | tf_op jit(solution)/shard_map/all_to_all | solution.py:74
  (132 shorter events, 38.6 us)
Async XLA Ops:
  1.8 10.2 %all-to-all-start = ((f32[1,2,4,32,256]{4,2,1,0,3:T(4,128)}), f32[1,2,4,32,256]{4,2,1,0,3:T(4,128)S(1)}, u32[]{:S(2)}, u32[]{:S(2)}) async-start(f32[1,2,4,32,256]{4,2,1,0,3:T(4,128)} %copy.6), calls=%async_computation | async-start | bytes 524288 | tf_op jit(solution)/shard_map/all_to_all | solution.py:29
  12.2 5.9 %collective-permute-start.1 = (bf16[2,2,8,1024]{3,2,1,0:T(8,128)(2,1)S(1)}, bf16[2,2,8,1024]{3,2,1,0:T(8,128)(2,1)S(1)}, u32[]{:S(2)}, u32[]{:S(2)}) collective-permute-start(bf16[2,2,8,1024]{3,2,1,0:T(8,128)(2,1)S(1)} %broadcast_select_fusion.2), channel_id=1, source_target_pairs={{0,4},{4,8},{8,12},{12,16},{16,20},{20,24},{24,28},{1,5},{5,9},{9,... | collective-permute-start | bytes 196616 | tf_op jit(solution)/shard_map/while/body/eval_jaxpr/ppermute | solution.py:10
  21.4 6.2 %collective-permute-start.1 = (bf16[2,2,8,1024]{3,2,1,0:T(8,128)(2,1)S(1)}, bf16[2,2,8,1024]{3,2,1,0:T(8,128)(2,1)S(1)}, u32[]{:S(2)}, u32[]{:S(2)}) collective-permute-start(bf16[2,2,8,1024]{3,2,1,0:T(8,128)(2,1)S(1)} %broadcast_select_fusion.2), channel_id=1, source_target_pairs={{0,4},{4,8},{8,12},{12,16},{16,20},{20,24},{24,28},{1,5},{5,9},{9,... | collective-permute-start | bytes 196616 | tf_op jit(solution)/shard_map/while/body/eval_jaxpr/ppermute | solution.py:10
  30.7 6.2 %collective-permute-start.1 = (bf16[2,2,8,1024]{3,2,1,0:T(8,128)(2,1)S(1)}, bf16[2,2,8,1024]{3,2,1,0:T(8,128)(2,1)S(1)}, u32[]{:S(2)}, u32[]{:S(2)}) collective-permute-start(bf16[2,2,8,1024]{3,2,1,0:T(8,128)(2,1)S(1)} %broadcast_select_fusion.2), channel_id=1, source_target_pairs={{0,4},{4,8},{8,12},{12,16},{16,20},{20,24},{24,28},{1,5},{5,9},{9,... | collective-permute-start | bytes 196616 | tf_op jit(solution)/shard_map/while/body/eval_jaxpr/ppermute | solution.py:10
  40.2 7.1 %collective-permute-start.1 = (bf16[2,2,8,1024]{3,2,1,0:T(8,128)(2,1)S(1)}, bf16[2,2,8,1024]{3,2,1,0:T(8,128)(2,1)S(1)}, u32[]{:S(2)}, u32[]{:S(2)}) collective-permute-start(bf16[2,2,8,1024]{3,2,1,0:T(8,128)(2,1)S(1)} %broadcast_select_fusion.2), channel_id=1, source_target_pairs={{0,4},{4,8},{8,12},{12,16},{16,20},{20,24},{24,28},{1,5},{5,9},{9,... | collective-permute-start | bytes 196616 | tf_op jit(solution)/shard_map/while/body/eval_jaxpr/ppermute | solution.py:10
  50.4 7.1 %collective-permute-start.1 = (bf16[2,2,8,1024]{3,2,1,0:T(8,128)(2,1)S(1)}, bf16[2,2,8,1024]{3,2,1,0:T(8,128)(2,1)S(1)}, u32[]{:S(2)}, u32[]{:S(2)}) collective-permute-start(bf16[2,2,8,1024]{3,2,1,0:T(8,128)(2,1)S(1)} %broadcast_select_fusion.2), channel_id=1, source_target_pairs={{0,4},{4,8},{8,12},{12,16},{16,20},{20,24},{24,28},{1,5},{5,9},{9,... | collective-permute-start | bytes 196616 | tf_op jit(solution)/shard_map/while/body/eval_jaxpr/ppermute | solution.py:10
  60.7 7.1 %collective-permute-start.1 = (bf16[2,2,8,1024]{3,2,1,0:T(8,128)(2,1)S(1)}, bf16[2,2,8,1024]{3,2,1,0:T(8,128)(2,1)S(1)}, u32[]{:S(2)}, u32[]{:S(2)}) collective-permute-start(bf16[2,2,8,1024]{3,2,1,0:T(8,128)(2,1)S(1)} %broadcast_select_fusion.2), channel_id=1, source_target_pairs={{0,4},{4,8},{8,12},{12,16},{16,20},{20,24},{24,28},{1,5},{5,9},{9,... | collective-permute-start | bytes 196616 | tf_op jit(solution)/shard_map/while/body/eval_jaxpr/ppermute | solution.py:10
  71.0 7.1 %collective-permute-start.1 = (bf16[2,2,8,1024]{3,2,1,0:T(8,128)(2,1)S(1)}, bf16[2,2,8,1024]{3,2,1,0:T(8,128)(2,1)S(1)}, u32[]{:S(2)}, u32[]{:S(2)}) collective-permute-start(bf16[2,2,8,1024]{3,2,1,0:T(8,128)(2,1)S(1)} %broadcast_select_fusion.2), channel_id=1, source_target_pairs={{0,4},{4,8},{8,12},{12,16},{16,20},{20,24},{24,28},{1,5},{5,9},{9,... | collective-permute-start | bytes 196616 | tf_op jit(solution)/shard_map/while/body/eval_jaxpr/ppermute | solution.py:10
  81.2 7.6 %collective-permute-start.1 = (bf16[2,2,8,1024]{3,2,1,0:T(8,128)(2,1)S(1)}, bf16[2,2,8,1024]{3,2,1,0:T(8,128)(2,1)S(1)}, u32[]{:S(2)}, u32[]{:S(2)}) collective-permute-start(bf16[2,2,8,1024]{3,2,1,0:T(8,128)(2,1)S(1)} %broadcast_select_fusion.2), channel_id=1, source_target_pairs={{0,4},{4,8},{8,12},{12,16},{16,20},{20,24},{24,28},{1,5},{5,9},{9,... | collective-permute-start | bytes 196616 | tf_op jit(solution)/shard_map/while/body/eval_jaxpr/ppermute | solution.py:10
  92.0 6.8 %collective-permute-start.1 = (bf16[2,2,8,1024]{3,2,1,0:T(8,128)(2,1)S(1)}, bf16[2,2,8,1024]{3,2,1,0:T(8,128)(2,1)S(1)}, u32[]{:S(2)}, u32[]{:S(2)}) collective-permute-start(bf16[2,2,8,1024]{3,2,1,0:T(8,128)(2,1)S(1)} %broadcast_select_fusion.2), channel_id=1, source_target_pairs={{0,4},{4,8},{8,12},{12,16},{16,20},{20,24},{24,28},{1,5},{5,9},{9,... | collective-permute-start | bytes 196616 | tf_op jit(solution)/shard_map/while/body/eval_jaxpr/ppermute | solution.py:10
  102.1 7.5 %collective-permute-start = (bf16[2,2,8,1024]{3,2,1,0:T(8,128)(2,1)S(1)}, bf16[2,2,8,1024]{3,2,1,0:T(8,128)(2,1)S(1)}, u32[]{:S(2)}, u32[]{:S(2)}) collective-permute-start(bf16[2,2,8,1024]{3,2,1,0:T(8,128)(2,1)S(1)} %get-tuple-element.559), channel_id=1, source_target_pairs={{4,0},{8,4},{12,8},{16,12},{20,16},{24,20},{28,24},{5,1},{9,5},{13... | collective-permute-start | bytes 196616 | tf_op jit(solution)/shard_map/while/body/eval_jaxpr/ppermute | solution.py:10
  112.8 7.4 %collective-permute-start = (bf16[2,2,8,1024]{3,2,1,0:T(8,128)(2,1)S(1)}, bf16[2,2,8,1024]{3,2,1,0:T(8,128)(2,1)S(1)}, u32[]{:S(2)}, u32[]{:S(2)}) collective-permute-start(bf16[2,2,8,1024]{3,2,1,0:T(8,128)(2,1)S(1)} %get-tuple-element.559), channel_id=1, source_target_pairs={{4,0},{8,4},{12,8},{16,12},{20,16},{24,20},{28,24},{5,1},{9,5},{13... | collective-permute-start | bytes 196616 | tf_op jit(solution)/shard_map/while/body/eval_jaxpr/ppermute | solution.py:10
  123.4 7.1 %collective-permute-start = (bf16[2,2,8,1024]{3,2,1,0:T(8,128)(2,1)S(1)}, bf16[2,2,8,1024]{3,2,1,0:T(8,128)(2,1)S(1)}, u32[]{:S(2)}, u32[]{:S(2)}) collective-permute-start(bf16[2,2,8,1024]{3,2,1,0:T(8,128)(2,1)S(1)} %get-tuple-element.559), channel_id=1, source_target_pairs={{4,0},{8,4},{12,8},{16,12},{20,16},{24,20},{28,24},{5,1},{9,5},{13... | collective-permute-start | bytes 196616 | tf_op jit(solution)/shard_map/while/body/eval_jaxpr/ppermute | solution.py:10
  133.6 7.1 %collective-permute-start = (bf16[2,2,8,1024]{3,2,1,0:T(8,128)(2,1)S(1)}, bf16[2,2,8,1024]{3,2,1,0:T(8,128)(2,1)S(1)}, u32[]{:S(2)}, u32[]{:S(2)}) collective-permute-start(bf16[2,2,8,1024]{3,2,1,0:T(8,128)(2,1)S(1)} %get-tuple-element.559), channel_id=1, source_target_pairs={{4,0},{8,4},{12,8},{16,12},{20,16},{24,20},{28,24},{5,1},{9,5},{13... | collective-permute-start | bytes 196616 | tf_op jit(solution)/shard_map/while/body/eval_jaxpr/ppermute | solution.py:10
  143.9 7.1 %collective-permute-start = (bf16[2,2,8,1024]{3,2,1,0:T(8,128)(2,1)S(1)}, bf16[2,2,8,1024]{3,2,1,0:T(8,128)(2,1)S(1)}, u32[]{:S(2)}, u32[]{:S(2)}) collective-permute-start(bf16[2,2,8,1024]{3,2,1,0:T(8,128)(2,1)S(1)} %get-tuple-element.559), channel_id=1, source_target_pairs={{4,0},{8,4},{12,8},{16,12},{20,16},{24,20},{28,24},{5,1},{9,5},{13... | collective-permute-start | bytes 196616 | tf_op jit(solution)/shard_map/while/body/eval_jaxpr/ppermute | solution.py:10
  154.1 7.1 %collective-permute-start = (bf16[2,2,8,1024]{3,2,1,0:T(8,128)(2,1)S(1)}, bf16[2,2,8,1024]{3,2,1,0:T(8,128)(2,1)S(1)}, u32[]{:S(2)}, u32[]{:S(2)}) collective-permute-start(bf16[2,2,8,1024]{3,2,1,0:T(8,128)(2,1)S(1)} %get-tuple-element.559), channel_id=1, source_target_pairs={{4,0},{8,4},{12,8},{16,12},{20,16},{24,20},{28,24},{5,1},{9,5},{13... | collective-permute-start | bytes 196616 | tf_op jit(solution)/shard_map/while/body/eval_jaxpr/ppermute | solution.py:10
  164.3 7.3 %collective-permute-start = (bf16[2,2,8,1024]{3,2,1,0:T(8,128)(2,1)S(1)}, bf16[2,2,8,1024]{3,2,1,0:T(8,128)(2,1)S(1)}, u32[]{:S(2)}, u32[]{:S(2)}) collective-permute-start(bf16[2,2,8,1024]{3,2,1,0:T(8,128)(2,1)S(1)} %get-tuple-element.559), channel_id=1, source_target_pairs={{4,0},{8,4},{12,8},{16,12},{20,16},{24,20},{28,24},{5,1},{9,5},{13... | collective-permute-start | bytes 196616 | tf_op jit(solution)/shard_map/while/body/eval_jaxpr/ppermute | solution.py:10
  174.8 7.3 %collective-permute-start = (bf16[2,2,8,1024]{3,2,1,0:T(8,128)(2,1)S(1)}, bf16[2,2,8,1024]{3,2,1,0:T(8,128)(2,1)S(1)}, u32[]{:S(2)}, u32[]{:S(2)}) collective-permute-start(bf16[2,2,8,1024]{3,2,1,0:T(8,128)(2,1)S(1)} %get-tuple-element.559), channel_id=1, source_target_pairs={{4,0},{8,4},{12,8},{16,12},{20,16},{24,20},{28,24},{5,1},{9,5},{13... | collective-permute-start | bytes 196616 | tf_op jit(solution)/shard_map/while/body/eval_jaxpr/ppermute | solution.py:10
  185.2 7.1 %collective-permute-start = (bf16[2,2,8,1024]{3,2,1,0:T(8,128)(2,1)S(1)}, bf16[2,2,8,1024]{3,2,1,0:T(8,128)(2,1)S(1)}, u32[]{:S(2)}, u32[]{:S(2)}) collective-permute-start(bf16[2,2,8,1024]{3,2,1,0:T(8,128)(2,1)S(1)} %get-tuple-element.559), channel_id=1, source_target_pairs={{4,0},{8,4},{12,8},{16,12},{20,16},{24,20},{28,24},{5,1},{9,5},{13... | collective-permute-start | bytes 196616 | tf_op jit(solution)/shard_map/while/body/eval_jaxpr/ppermute | solution.py:10
where the time goes:
time: 234 us; the launch traced here: 232 us
  waiting for transfers between devices  63.5 us (27%)
  starting transfers between devices  59.3 us (25%)
  matrix products  53.7 us (23%)
  local copies, waits for them, and re-layouts  41 us (18%)
  blocking collectives  8.42 us (4%)
  other arithmetic  4.25 us (2%)
    ppermute x18, waiting for transfers between devices, from_behind(): lax.ppermute(value, axis, [(source, source + steps) for source in range(f...  57.5 us
    ppermute x18, starting transfers between devices, from_behind(): lax.ppermute(value, axis, [(source, source + steps) for source in range(f...  55 us
    dot_general x18, matrix products, complex_product(): product = jnp.dot(flat, inverse, preferred_element_type=jnp.float32)  53.7 us
    unnamed x4, local copies, waits for them, and re-layouts  20.1 us
    mul x18, local copies, waits for them, and re-layouts, twist(): real = factor[0] * field[0] - factor[1] * field[1]  12.8 us
    all_to_all x1, blocking collectives, body(): lax.all_to_all(backward_store[None], 'plane', split_axis=4, concat_axis=3...  8.42 us
    all_to_all x1, waiting for transfers between devices, body(): lax.all_to_all(rhs_field, 'plane', split_axis=3, concat_axis=4, tiled=True)  6.04 us
    all_to_all x2, local copies, waits for them, and re-layouts, body(): lax.all_to_all(backward_store[None], 'plane', split_axis=4, concat_axis=3...  4.9 us
  transfers between devices with their start and end apart: 19, of which 19 were waited for; matrix products, arithmetic and copies ran while one was open for 6% of the time, Pallas kernels for 0%

commit v1 on v0

v1 whole, which is shorter than its diff:
```python
import functools

import jax
import jax.numpy as jnp
from jax import lax
from jax.experimental import pallas as pl
from jax.experimental.pallas import tpu as pltpu
from jax.sharding import PartitionSpec as P

MESH = pl.DeviceIdType.MESH
GROUP = 1


def kernel(layers, planes, rhs, inverse_hbm, coupling, out, inverse, stage, lines, factors, ahead, ahead_out,
           behind, behind_out, forward, out_stage, out_in, inverse_sem, in_send, in_recv, ahead_send, ahead_recv,
           behind_send, behind_recv, out_send, out_recv):
    place = lax.axis_index("layer")
    mine = lax.axis_index("plane")
    last = layers - 1
    loads = rhs.shape[2]
    cells = coupling.shape[3]
    width = inverse.shape[0]
    part = rhs.shape[4]
    rows = 2 * cells
    blocks = loads // GROUP

    load_inverse = pltpu.make_async_copy(inverse_hbm.at[0], inverse, inverse_sem)
    load_inverse.start()

    barrier = pltpu.get_barrier_semaphore()
    peers = [lax.rem(mine + s, planes) for s in range(1, planes)]
    for peer in peers:
        pl.semaphore_signal(barrier, inc=1, device_id=(place, peer), device_id_type=MESH)

    @pl.when(place > 0)
    def _():
        pl.semaphore_signal(barrier, inc=1, device_id=(place - 1, mine), device_id_type=MESH)

    @pl.when(place < last)
    def _():
        pl.semaphore_signal(barrier, inc=1, device_id=(place + 1, mine), device_id_type=MESH)

    for p in range(planes):
        for r in range(loads):
            piece = rhs[0, :, r, p * cells:(p + 1) * cells, :].reshape(rows, part)
            stage[p, r] = piece.astype(jnp.bfloat16)

    @pl.when(place == 0)
    def _():
        ahead[...] = jnp.zeros_like(ahead)

    eye = lax.broadcasted_iota(jnp.int32, (cells, cells), 0) == lax.broadcasted_iota(jnp.int32, (cells, cells), 1)
    for c in range(2):
        for r in range(loads):
            row = jnp.broadcast_to(coupling[0, c, r:r + 1, :], (cells, cells))
            column = jnp.sum(jnp.where(eye, row, 0.0), axis=1, keepdims=True)
            factors[c, r] = jnp.broadcast_to(column, (cells, 128))

    pl.semaphore_wait(barrier, planes - 1 + jnp.where(place > 0, 1, 0) + jnp.where(place < last, 1, 0))

    def spread(r, s, source, target, send, recv):
        return pltpu.make_async_remote_copy(
            src_ref=source.at[peers[s], r], dst_ref=target.at[mine, r],
            send_sem=send.at[r, s], recv_sem=recv.at[r, s],
            device_id=(place, peers[s]), device_id_type=MESH)

    def sweep(b, source, target, send, recv, step):
        return pltpu.make_async_remote_copy(
            src_ref=source.at[b], dst_ref=target.at[b],
            send_sem=send.at[b], recv_sem=recv.at[b],
            device_id=(place + step, mine), device_id_type=MESH)

    for r in range(loads):
        for s in range(planes - 1):
            spread(r, s, stage, lines, in_send, in_recv).start()
        lines[mine, r] = stage[mine, r]

    def product(operand):
        flat = jnp.dot(operand, inverse[...], preferred_element_type=jnp.float32)
        flat = flat.reshape(GROUP, 2, cells, 2 * width)
        real = flat[:, 0, :, :width] - flat[:, 1, :, width:]
        imag = flat[:, 0, :, width:] + flat[:, 1, :, :width]
        return real, imag

    def pack(real, imag):
        return jnp.stack([real, imag], axis=1).reshape(GROUP * rows, width)

    def twist(b, real, imag):
        group = pl.ds(b * GROUP, GROUP)
        a = jnp.tile(factors[0, group], (1, 1, width // 128))
        c = jnp.tile(factors[1, group], (1, 1, width // 128))
        return a * real - c * imag, a * imag + c * real

    def split(flat):
        parts = flat.astype(jnp.float32).reshape(GROUP, 2, cells, width)
        return parts[:, 0], parts[:, 1]

    def finish(b, field):
        for r in range(b * GROUP, (b + 1) * GROUP):
            at = (r - b * GROUP) * rows
            for p in range(planes):
                out_stage[p, r] = field[at:at + rows, p * part:(p + 1) * part].astype(jnp.bfloat16)
            for s in range(planes - 1):
                spread(r, s, out_stage, out_in, out_send, out_recv).start()

    for b in range(blocks):
        for r in range(b * GROUP, (b + 1) * GROUP):
            for s in range(planes - 1):
                spread(r, s, stage, lines, in_send, in_recv).wait_recv()
        source = jnp.concatenate(
            [lines[p, b * GROUP:(b + 1) * GROUP].reshape(GROUP * rows, part) for p in range(planes)], axis=1)
        source_real, source_imag = split(source)

        @pl.when(place > 0)
        def _():
            sweep(b, ahead_out, ahead, ahead_send, ahead_recv, 1).wait_recv()

        real, imag = twist(b, *split(ahead[b]))
        mixed = pack(source_real + real, source_imag + imag).astype(jnp.bfloat16)
        if b == 0:
            load_inverse.wait()
        real, imag = product(mixed)
        result = pack(real, imag)
        forward[b] = result

        @pl.when(place < last)
        def _():
            ahead_out[b] = result.astype(jnp.bfloat16)
            sweep(b, ahead_out, ahead, ahead_send, ahead_recv, 1).start()

        @pl.when(place == last)
        def _():
            behind_out[b] = pack(*twist(b, real, imag)).astype(jnp.bfloat16)
            sweep(b, behind_out, behind, behind_send, behind_recv, -1).start()
            finish(b, result)

    @pl.when(place < last)
    def _():
        for b in range(blocks):
            first_real, first_imag = split(forward[b])
            sweep(b, behind_out, behind, behind_send, behind_recv, -1).wait_recv()
            real, imag = product(behind[b])
            real, imag = first_real + real, first_imag + imag

            @pl.when(place > 0)
            def _():
                behind_out[b] = pack(*twist(b, real, imag)).astype(jnp.bfloat16)
                sweep(b, behind_out, behind, behind_send, behind_recv, -1).start()

            finish(b, pack(real, imag))

    out_in[mine] = out_stage[mine]
    for r in range(loads):
        for s in range(planes - 1):
            spread(r, s, out_stage, out_in, out_send, out_recv).wait_recv()
        for p in range(planes):
            out[0, :, r, p * cells:(p + 1) * cells, :] = out_in[p, r].astype(jnp.float32).reshape(2, cells, part)

    for r in range(loads):
        for s in range(planes - 1):
            spread(r, s, stage, lines, in_send, in_recv).wait_send()
            spread(r, s, out_stage, out_in, out_send, out_recv).wait_send()

    @pl.when(place < last)
    def _():
        for b in range(blocks):
            sweep(b, ahead_out, ahead, ahead_send, ahead_recv, 1).wait_send()

    @pl.when(place > 0)
    def _():
        for b in range(blocks):
            sweep(b, behind_out, behind, behind_send, behind_recv, -1).wait_send()


def body(rhs_field, panel_inverse, coupling):
    layers, planes = lax.axis_size("layer"), lax.axis_size("plane")
    loads, part = rhs_field.shape[2], rhs_field.shape[4]
    width = panel_inverse.shape[1]
    cells = coupling.shape[3]
    rows = 2 * cells
    blocks = loads // GROUP
    exchange = pltpu.VMEM((planes, loads, rows, part), jnp.bfloat16)
    hop = pltpu.VMEM((blocks, GROUP * rows, width), jnp.bfloat16)
    per_peer = pltpu.SemaphoreType.DMA((loads, planes - 1))
    per_block = pltpu.SemaphoreType.DMA((blocks,))
    vmem = pl.BlockSpec(memory_space=pltpu.VMEM)
    return pl.pallas_call(
        functools.partial(kernel, layers, planes),
        out_shape=jax.ShapeDtypeStruct(rhs_field.shape, jnp.float32),
        in_specs=[vmem, pl.BlockSpec(memory_space=pl.ANY), vmem],
        out_specs=vmem,
        scratch_shapes=[
            pltpu.VMEM(panel_inverse.shape[1:], jnp.bfloat16),
            exchange,
            exchange,
            pltpu.VMEM((2, loads, cells, 128), jnp.float32),
            hop,
            hop,
            hop,
            hop,
            pltpu.VMEM((blocks, GROUP * rows, width), jnp.float32),
            exchange,
            exchange,
            pltpu.SemaphoreType.DMA,
            per_peer,
            per_peer,
            per_block,
            per_block,
            per_block,
            per_block,
            per_peer,
            per_peer,
        ],
        compiler_params=pltpu.CompilerParams(
            collective_id=0, has_side_effects=True, vmem_limit_bytes=60 * 1024 * 1024),
    )(rhs_field, panel_inverse, coupling)


def solution(mesh):
    in_specs = (
        P("layer", None, None, None, "plane"),
        P("layer", None, None),
        P("layer", None, None, "plane"),
    )
    out_specs = P("layer", None, None, None, "plane")
    return jax.shard_map(body, mesh=mesh, in_specs=in_specs, out_specs=out_specs, check_vma=False)
```

time: 234 us -> 68.3 us (0.29)
  Pallas kernels: 0 us -> 66.5 us
  waiting for transfers between devices: 63.5 us -> 0 us
  starting transfers between devices: 59.3 us -> 0 us
  matrix products: 53.7 us -> 0 us
  local copies, waits for them, and re-layouts: 41 us -> 1.67 us
  blocking collectives: 8.42 us -> 0 us
  other arithmetic: 4.25 us -> 0 us
    pallas_call x0 -> x1, Pallas kernels: none -> 66.5 us  [body(): pl.pallas_call(functools.partial(kernel, layers, planes), out_shape=jax.S...]
    ppermute x18 -> x0, waiting for transfers between devices: 57.5 us -> none  [from_behind(): lax.ppermute(value, axis, [(source, source + steps) for source in range(f...]
    ppermute x18 -> x0, starting transfers between devices: 55 us -> none  [from_behind(): lax.ppermute(value, axis, [(source, source + steps) for source in range(f...]
    dot_general x18 -> x0, matrix products: 53.7 us -> none  [complex_product(): product = jnp.dot(flat, inverse, preferred_element_type=jnp.float32)]
    unnamed x4 -> x1, local copies, waits for them, and re-layouts: 20.1 us -> 1.67 us
    mul x18 -> x0, local copies, waits for them, and re-layouts: 12.8 us -> none  [twist(): real = factor[0] * field[0] - factor[1] * field[1]]
    all_to_all x1 -> x0, blocking collectives: 8.42 us -> none  [body(): lax.all_to_all(backward_store[None], 'plane', split_axis=4, concat_axis=3...]
    all_to_all x1 -> x0, waiting for transfers between devices: 6.04 us -> none  [body(): lax.all_to_all(rhs_field, 'plane', split_axis=3, concat_axis=4, tiled=True)]
  transfers between devices with their start and end apart: 19 -> 0, of which waited for: 19 -> 0; matrix products, arithmetic and copies ran while one was open for 6% -> 0% of each run, Pallas kernels for 0% -> 0%
where the time goes in v1:
time: 68.3 us; the launch traced here: 68.2 us
  Pallas kernels  66.5 us (97%)
  local copies, waits for them, and re-layouts  1.67 us (2%)
    pallas_call x1, Pallas kernels, body(): pl.pallas_call(functools.partial(kernel, layers, planes), out_shape=jax.S...  66.5 us
    unnamed x1, local copies, waits for them, and re-layouts  1.67 us

profile of v1, /device:TPU:0, one launch (start us, length us, event | category | flops | bytes accessed | tf_op | source)
XLA Modules:
  0.0 68.2 jit_solution(12474313274913220418)
XLA Ops:
  0.0 66.5 %shard_map.37 = f32[1,2,4,32,256]{4,3,2,1,0:T(8,128)} custom-call(f32[1,2,4,32,256]{4,3,2,1,0:T(8,128)} %rhs.1, bf16[1,1024,2048]{2,1,0:T(8,128)(2,1)} %inverse_hbm.1, f32[1,2,4,8]{3,2,1,0:T(4,128)} %coupling.1), custom_call_target="tpu_custom_call" | custom-call | tf_op jit(solution)/shard_map/pallas_call | solution.py:187
  66.5 1.7 %copy.5 = f32[1,2,4,32,256]{4,3,2,1,0:T(8,128)} copy(f32[1,2,4,32,256]{4,3,2,1,0:T(8,128)} %shard_map.37) | data formatting | bytes 524288

commit v2 on v1

v2 whole, which is shorter than its diff:
```python
import functools

import jax
import jax.numpy as jnp
from jax import lax
from jax.experimental import pallas as pl
from jax.experimental.pallas import tpu as pltpu
from jax.sharding import PartitionSpec as P

MESH = pl.DeviceIdType.MESH
CHUNKS = 2


def kernel(layers, planes, rhs, inverse_hbm, coupling, out, inverse, stage, lines, factors, ahead, ahead_out,
           behind, behind_out, forward, out_stage, out_in, inverse_sem, in_send, in_recv, ahead_send, ahead_recv,
           behind_send, behind_recv, out_send, out_recv):
    place = lax.axis_index("layer")
    mine = lax.axis_index("plane")
    last = layers - 1
    loads = rhs.shape[2]
    cells = coupling.shape[3]
    width = inverse.shape[0]
    part = rhs.shape[4]
    rows = 2 * cells

    load_inverse = pltpu.make_async_copy(inverse_hbm.at[0], inverse, inverse_sem)
    load_inverse.start()

    barrier = pltpu.get_barrier_semaphore()
    peers = [lax.rem(mine + s, planes) for s in range(1, planes)]
    for peer in peers:
        pl.semaphore_signal(barrier, inc=1, device_id=(place, peer), device_id_type=MESH)

    @pl.when(place > 0)
    def _():
        pl.semaphore_signal(barrier, inc=1, device_id=(place - 1, mine), device_id_type=MESH)

    @pl.when(place < last)
    def _():
        pl.semaphore_signal(barrier, inc=1, device_id=(place + 1, mine), device_id_type=MESH)

    for p in range(planes):
        for r in range(loads):
            piece = rhs[0, :, r, p * cells:(p + 1) * cells, :].reshape(rows, part)
            stage[p, r] = piece.astype(jnp.bfloat16)

    eye = lax.broadcasted_iota(jnp.int32, (cells, cells), 0) == lax.broadcasted_iota(jnp.int32, (cells, cells), 1)
    for c in range(2):
        for r in range(loads):
            row = jnp.broadcast_to(coupling[0, c, r:r + 1, :], (cells, cells))
            column = jnp.sum(jnp.where(eye, row, 0.0), axis=1, keepdims=True)
            factors[c, r] = jnp.broadcast_to(column, (cells, 128))

    pl.semaphore_wait(barrier, planes - 1 + jnp.where(place > 0, 1, 0) + jnp.where(place < last, 1, 0))

    def spread(r, s, source, target, send, recv):
        return pltpu.make_async_remote_copy(
            src_ref=source.at[peers[s], r], dst_ref=target.at[mine, r],
            send_sem=send.at[r, s], recv_sem=recv.at[r, s],
            device_id=(place, peers[s]), device_id_type=MESH)

    def sweep(b, n, source, target, send, recv, step):
        return pltpu.make_async_remote_copy(
            src_ref=source.at[b, n], dst_ref=target.at[b, n],
            send_sem=send.at[b, n], recv_sem=recv.at[b, n],
            device_id=(place + step, mine), device_id_type=MESH)

    def up(b, n):
        return sweep(b, n, ahead_out, ahead, ahead_send, ahead_recv, 1)

    def down(b, n):
        return sweep(b, n, behind_out, behind, behind_send, behind_recv, -1)

    for r in range(loads):
        for s in range(planes - 1):
            spread(r, s, stage, lines, in_send, in_recv).start()
        lines[mine, r] = stage[mine, r]

    chunk = width // CHUNKS

    def combine(left, right):
        real = left[:cells] - right[cells:]
        imag = right[:cells] + left[cells:]
        return real, imag

    def pack(real, imag):
        return jnp.concatenate([real, imag], axis=0)

    def dot(operand, k, start, size):
        return jnp.dot(operand, inverse[k * chunk:(k + 1) * chunk, start:start + size],
                       preferred_element_type=jnp.float32)

    def twist(b, real, imag):
        a = jnp.tile(factors[0, b], (1, chunk // 128))
        c = jnp.tile(factors[1, b], (1, chunk // 128))
        return a * real - c * imag, a * imag + c * real

    def product(source, b, copy, use):
        total = None
        for k in range(CHUNKS - 1):
            copy(b, k).wait_recv()
            term = dot(source[b, k], k, 0, 2 * width)
            total = term if total is None else total + term
        k = CHUNKS - 1
        copy(b, k).wait_recv()
        operand = source[b, k]
        for n in range(CHUNKS):
            left = dot(operand, k, n * chunk, chunk)
            right = dot(operand, k, width + n * chunk, chunk)
            if total is not None:
                left = total[:, n * chunk:(n + 1) * chunk] + left
                right = total[:, width + n * chunk:width + (n + 1) * chunk] + right
            use(n, *combine(left, right))

    def send_up(b, n, field):
        ahead_out[b, n] = field.astype(jnp.bfloat16)
        up(b, n).start()

    def send_down(b, n, real, imag):
        behind_out[b, n] = pack(*twist(b, real, imag)).astype(jnp.bfloat16)
        down(b, n).start()

    def keep(b, n, field):
        for p in range(n * chunk // part, (n + 1) * chunk // part):
            at = p * part - n * chunk
            out_stage[p, b] = field[:, at:at + part].astype(jnp.bfloat16)

    def finish(b):
        for s in range(planes - 1):
            spread(b, s, out_stage, out_in, out_send, out_recv).start()

    for b in range(loads):
        for s in range(planes - 1):
            spread(b, s, stage, lines, in_send, in_recv).wait_recv()
        if b == 0:
            load_inverse.wait()
        source = jnp.concatenate([lines[p, b] for p in range(planes)], axis=1)
        for n in range(CHUNKS):
            left = jnp.dot(source, inverse[:, n * chunk:(n + 1) * chunk], preferred_element_type=jnp.float32)
            right = jnp.dot(source, inverse[:, width + n * chunk:width + (n + 1) * chunk],
                            preferred_element_type=jnp.float32)
            field = pack(*combine(left, right))
            forward[b, n] = field

            @pl.when(place == 0)
            def _():
                send_up(b, n, field)

    @pl.when(place > 0)
    def _():
        for b in range(loads):
            def use(n, real, imag):
                real, imag = twist(b, real, imag)
                field = forward[b, n] + pack(real, imag)

                @pl.when(place < last)
                def _():
                    send_up(b, n, field)

                @pl.when(place == last)
                def _():
                    send_down(b, n, field[:cells], field[cells:])
                    keep(b, n, field)

                forward[b, n] = field

            product(ahead, b, up, use)

            @pl.when(place == last)
            def _():
                finish(b)

    @pl.when(place < last)
    def _():
        for b in range(loads):
            def use(n, real, imag):
                field = forward[b, n] + pack(real, imag)

                @pl.when(place > 0)
                def _():
                    send_down(b, n, field[:cells], field[cells:])

                keep(b, n, field)

            product(behind, b, down, use)
            finish(b)

    out_in[mine] = out_stage[mine]
    for r in range(loads):
        for s in range(planes - 1):
            spread(r, s, out_stage, out_in, out_send, out_recv).wait_recv()
        for p in range(planes):
            out[0, :, r, p * cells:(p + 1) * cells, :] = out_in[p, r].astype(jnp.float32).reshape(2, cells, part)

    for r in range(loads):
        for s in range(planes - 1):
            spread(r, s, stage, lines, in_send, in_recv).wait_send()
            spread(r, s, out_stage, out_in, out_send, out_recv).wait_send()

    @pl.when(place < last)
    def _():
        for b in range(loads):
            for n in range(CHUNKS):
                up(b, n).wait_send()

    @pl.when(place > 0)
    def _():
        for b in range(loads):
            for n in range(CHUNKS):
                down(b, n).wait_send()


def body(rhs_field, panel_inverse, coupling):
    layers, planes = lax.axis_size("layer"), lax.axis_size("plane")
    loads, part = rhs_field.shape[2], rhs_field.shape[4]
    width = panel_inverse.shape[1]
    cells = coupling.shape[3]
    rows = 2 * cells
    exchange = pltpu.VMEM((planes, loads, rows, part), jnp.bfloat16)
    hop = pltpu.VMEM((loads, CHUNKS, rows, width // CHUNKS), jnp.bfloat16)
    per_peer = pltpu.SemaphoreType.DMA((loads, planes - 1))
    per_block = pltpu.SemaphoreType.DMA((loads, CHUNKS))
    vmem = pl.BlockSpec(memory_space=pltpu.VMEM)
    return pl.pallas_call(
        functools.partial(kernel, layers, planes),
        out_shape=jax.ShapeDtypeStruct(rhs_field.shape, jnp.float32),
        in_specs=[vmem, pl.BlockSpec(memory_space=pl.ANY), vmem],
        out_specs=vmem,
        scratch_shapes=[
            pltpu.VMEM(panel_inverse.shape[1:], jnp.bfloat16),
            exchange,
            exchange,
            pltpu.VMEM((2, loads, cells, 128), jnp.float32),
            hop,
            hop,
            hop,
            hop,
            pltpu.VMEM((loads, CHUNKS, rows, width // CHUNKS), jnp.float32),
            exchange,
            exchange,
            pltpu.SemaphoreType.DMA,
            per_peer,
            per_peer,
            per_block,
            per_block,
            per_block,
            per_block,
            per_peer,
            per_peer,
        ],
        compiler_params=pltpu.CompilerParams(
            collective_id=0, has_side_effects=True, vmem_limit_bytes=60 * 1024 * 1024),
    )(rhs_field, panel_inverse, coupling)


def solution(mesh):
    in_specs = (
        P("layer", None, None, None, "plane"),
        P("layer", None, None),
        P("layer", None, None, "plane"),
    )
    out_specs = P("layer", None, None, None, "plane")
    return jax.shard_map(body, mesh=mesh, in_specs=in_specs, out_specs=out_specs, check_vma=False)
```

time: 68.3 us -> 65.1 us (0.953)
  Pallas kernels: 66.5 us -> 63.2 us
    pallas_call x1, Pallas kernels: 66.5 us -> 63.2 us  [body(): pl.pallas_call(functools.partial(kernel, layers, planes), out_shape=jax.S...]
where the time goes in v2:
time: 65.1 us; the launch traced here: 64.9 us
  Pallas kernels  63.2 us (97%)
  local copies, waits for them, and re-layouts  1.67 us (3%)
    pallas_call x1, Pallas kernels, body(): pl.pallas_call(functools.partial(kernel, layers, planes), out_shape=jax.S...  63.2 us
    unnamed x1, local copies, waits for them, and re-layouts  1.67 us

profile of v2, /device:TPU:0, one launch (start us, length us, event | category | flops | bytes accessed | tf_op | source)
XLA Modules:
  0.0 64.9 jit_solution(16997566186335805922)
XLA Ops:
  0.0 63.2 %shard_map.37 = f32[1,2,4,32,256]{4,3,2,1,0:T(8,128)} custom-call(f32[1,2,4,32,256]{4,3,2,1,0:T(8,128)} %rhs.1, bf16[1,1024,2048]{2,1,0:T(8,128)(2,1)} %inverse_hbm.1, f32[1,2,4,8]{3,2,1,0:T(4,128)} %coupling.1), custom_call_target="tpu_custom_call" | custom-call | tf_op jit(solution)/shard_map/pallas_call | solution.py:224
  63.2 1.7 %copy.5 = f32[1,2,4,32,256]{4,3,2,1,0:T(8,128)} copy(f32[1,2,4,32,256]{4,3,2,1,0:T(8,128)} %shard_map.37) | data formatting | bytes 524288

commit v3 on v2

--- a/solution.py
+++ b/solution.py
@@ -11,8 +11,8 @@
 CHUNKS = 2
 
 
-def kernel(layers, planes, rhs, inverse_hbm, coupling, out, inverse, stage, lines, factors, ahead, ahead_out,
-           behind, behind_out, forward, out_stage, out_in, inverse_sem, in_send, in_recv, ahead_send, ahead_recv,
+def kernel(layers, planes, rhs_hbm, inverse_hbm, coupling_hbm, out, rhs, coupling, inverse, stage, lines, factors, ahead, ahead_out,
+           behind, behind_out, forward, out_stage, out_in, load_sem, in_send, in_recv, ahead_send, ahead_recv,
            behind_send, behind_recv, out_send, out_recv):
     place = lax.axis_index("layer")
     mine = lax.axis_index("plane")
@@ -23,7 +23,11 @@
     part = rhs.shape[4]
     rows = 2 * cells
 
-    load_inverse = pltpu.make_async_copy(inverse_hbm.at[0], inverse, inverse_sem)
+    load_rhs = pltpu.make_async_copy(rhs_hbm, rhs, load_sem.at[0])
+    load_coupling = pltpu.make_async_copy(coupling_hbm, coupling, load_sem.at[1])
+    load_inverse = pltpu.make_async_copy(inverse_hbm.at[0], inverse, load_sem.at[2])
+    load_rhs.start()
+    load_coupling.start()
     load_inverse.start()
 
     barrier = pltpu.get_barrier_semaphore()
@@ -39,17 +43,11 @@
     def _():
         pl.semaphore_signal(barrier, inc=1, device_id=(place + 1, mine), device_id_type=MESH)
 
+    load_rhs.wait()
     for p in range(planes):
         for r in range(loads):
             piece = rhs[0, :, r, p * cells:(p + 1) * cells, :].reshape(rows, part)
             stage[p, r] = piece.astype(jnp.bfloat16)
-
-    eye = lax.broadcasted_iota(jnp.int32, (cells, cells), 0) == lax.broadcasted_iota(jnp.int32, (cells, cells), 1)
-    for c in range(2):
-        for r in range(loads):
-            row = jnp.broadcast_to(coupling[0, c, r:r + 1, :], (cells, cells))
-            column = jnp.sum(jnp.where(eye, row, 0.0), axis=1, keepdims=True)
-            factors[c, r] = jnp.broadcast_to(column, (cells, 128))
 
     pl.semaphore_wait(barrier, planes - 1 + jnp.where(place > 0, 1, 0) + jnp.where(place < last, 1, 0))
 
@@ -129,6 +127,14 @@
         for s in range(planes - 1):
             spread(b, s, out_stage, out_in, out_send, out_recv).start()
 
+    load_coupling.wait()
+    eye = lax.broadcasted_iota(jnp.int32, (cells, cells), 0) == lax.broadcasted_iota(jnp.int32, (cells, cells), 1)
+    for c in range(2):
+        for r in range(loads):
+            row = jnp.broadcast_to(coupling[0, c, r:r + 1, :], (cells, cells))
+            column = jnp.sum(jnp.where(eye, row, 0.0), axis=1, keepdims=True)
+            factors[c, r] = jnp.broadcast_to(column, (cells, 128))
+
     for b in range(loads):
         for s in range(planes - 1):
             spread(b, s, stage, lines, in_send, in_recv).wait_recv()
@@ -146,41 +152,43 @@
             def _():
                 send_up(b, n, field)
 
-    @pl.when(place > 0)
-    def _():
-        for b in range(loads):
-            def use(n, real, imag):
-                real, imag = twist(b, real, imag)
+    @pl.when((place > 0) & (place < last))
+    def _():
+        for b in range(loads):
+            def use(n, real, imag):
+                field = forward[b, n] + pack(*twist(b, real, imag))
+                send_up(b, n, field)
+                forward[b, n] = field
+
+            product(ahead, b, up, use)
+
+    @pl.when(place == last)
+    def _():
+        for b in range(loads):
+            def use(n, real, imag):
+                field = forward[b, n] + pack(*twist(b, real, imag))
+                send_down(b, n, field[:cells], field[cells:])
+                keep(b, n, field)
+
+            product(ahead, b, up, use)
+            finish(b)
+
+    @pl.when((place > 0) & (place < last))
+    def _():
+        for b in range(loads):
+            def use(n, real, imag):
                 field = forward[b, n] + pack(real, imag)
-
-                @pl.when(place < last)
-                def _():
-                    send_up(b, n, field)
-
-                @pl.when(place == last)
-                def _():
-                    send_down(b, n, field[:cells], field[cells:])
-                    keep(b, n, field)
-
-                forward[b, n] = field
-
-            product(ahead, b, up, use)
-
-            @pl.when(place == last)
-            def _():
-                finish(b)
-
-    @pl.when(place < last)
-    def _():
-        for b in range(loads):
-            def use(n, real, imag):
-                field = forward[b, n] + pack(real, imag)
-
-                @pl.when(place > 0)
-                def _():
-                    send_down(b, n, field[:cells], field[cells:])
-
+                send_down(b, n, field[:cells], field[cells:])
                 keep(b, n, field)
+
+            product(behind, b, down, use)
+            finish(b)
+
+    @pl.when(place == 0)
+    def _():
+        for b in range(loads):
+            def use(n, real, imag):
+                keep(b, n, forward[b, n] + pack(real, imag))
 
             product(behind, b, down, use)
             finish(b)
@@ -224,9 +232,11 @@
     return pl.pallas_call(
         functools.partial(kernel, layers, planes),
         out_shape=jax.ShapeDtypeStruct(rhs_field.shape, jnp.float32),
-        in_specs=[vmem, pl.BlockSpec(memory_space=pl.ANY), vmem],
+        in_specs=[pl.BlockSpec(memory_space=pl.ANY)] * 3,
         out_specs=vmem,
         scratch_shapes=[
+            pltpu.VMEM(rhs_field.shape, jnp.float32),
+            pltpu.VMEM(coupling.shape, jnp.float32),
             pltpu.VMEM(panel_inverse.shape[1:], jnp.bfloat16),
             exchange,
             exchange,
@@ -238,7 +248,7 @@
             pltpu.VMEM((loads, CHUNKS, rows, width // CHUNKS), jnp.float32),
             exchange,
             exchange,
-            pltpu.SemaphoreType.DMA,
+            pltpu.SemaphoreType.DMA((3,)),
             per_peer,
             per_peer,
             per_block,

time: 65.1 us -> 64 us (0.983)
  Pallas kernels: 63.2 us -> 62.2 us
    pallas_call x1, Pallas kernels: 63.2 us -> 62.2 us  [body(): pl.pallas_call(functools.partial(kernel, layers, planes), out_shape=jax.S...]
where the time goes in v3:
time: 64 us; the launch traced here: 63.8 us
  Pallas kernels  62.2 us (97%)
  local copies, waits for them, and re-layouts  1.67 us (3%)
    pallas_call x1, Pallas kernels, body(): pl.pallas_call(functools.partial(kernel, layers, planes), out_shape=jax.S...  62.2 us
    unnamed x1, local copies, waits for them, and re-layouts  1.67 us

profile of v3, /device:TPU:0, one launch (start us, length us, event | category | flops | bytes accessed | tf_op | source)
XLA Modules:
  0.0 63.8 jit_solution(10632976189754804543)
XLA Ops:
  0.0 62.2 %shard_map.37 = f32[1,2,4,32,256]{4,3,2,1,0:T(8,128)} custom-call(f32[1,2,4,32,256]{4,3,2,1,0:T(8,128)} %rhs_hbm.1, bf16[1,1024,2048]{2,1,0:T(8,128)(2,1)} %inverse_hbm.1, f32[1,2,4,8]{3,2,1,0:T(4,128)} %coupling_hbm.1), custom_call_target="tpu_custom_call" | custom-call | tf_op jit(solution)/shard_map/pallas_call | solution.py:232
  62.2 1.7 %copy.5 = f32[1,2,4,32,256]{4,3,2,1,0:T(8,128)} copy(f32[1,2,4,32,256]{4,3,2,1,0:T(8,128)} %shard_map.37) | data formatting | bytes 524288
